TPU v7x, 128 devices: a whole 4x4x4 slice. The times are simulated.
128 devices in a mesh: gx: 16 (over x, y), gy: 8 (over z, core).
Axes of the slice: x: 4, y: 4, z: 4, core: 2. Of those that a mesh axis runs over, the one named last changes fastest.
Arguments:
- theta: float32 [10, 128, 128, 128], P(None, 'gx', 'gy'), may hold values from -6 to 6
- phi_table: float32 [1024, 100], replicated, may hold values from -0.1 to 0.3
- dphi_table: float32 [1024, 100], replicated, may hold values from -0.5 to 1
Outputs:
- u_grids: float32 [10, 128, 128, 128], P(None, 'gx', 'gy')
- stress: float32 [3, 3], replicated
- energy: float32 [], replicated
All inputs are finite; a program needn't handle non-finite values.
Results may differ from a plain program's by a relative error of at most 0.0003.
Values sent between devices are 32-bit elements; how exact they have to be, the bound alone decides.
A program may use at most 64 MiB of HBM per device.

v0:
```python
import functools
import math

import jax
import jax.numpy as jnp
import ml_dtypes
import numpy as np
from jax import lax
from jax.experimental import pallas as pl
from jax.experimental.pallas import tpu as pltpu
from jax.sharding import PartitionSpec as P

MESH = pl.DeviceIdType.MESH
F32 = jnp.float32
BF16 = jnp.bfloat16
N = 128
HALF = 64
Q = 10
GX = 16
GY = 8
NC = 5
NQ = Q // NC
PAIRS = 160
KROWS = 72
TABLE = 1024


def real_basis():
    r = np.arange(N)
    rows = [np.full(N, 1.0) / np.sqrt(N)]
    rows += [np.cos(2 * np.pi * k * r / N) * np.sqrt(2.0 / N) for k in range(1, HALF)]
    rows += [np.cos(np.pi * r) / np.sqrt(N)]
    rows += [np.sin(2 * np.pi * k * r / N) * np.sqrt(2.0 / N) for k in range(1, HALF)]
    return np.array(rows)


def halves(array):
    high = array.astype(ml_dtypes.bfloat16)
    low = (array - high.astype(np.float64)).astype(ml_dtypes.bfloat16)
    return np.stack([high, low])


def sym_index(q, p):
    q, p = min(q, p), max(q, p)
    return 100 + q * Q - q * (q - 1) // 2 + (p - q)


def constants():
    basis = real_basis()
    order = np.array([(lane // 2) + HALF * (lane % 2) for lane in range(N)])
    z_basis = basis[order]
    pick = np.zeros((2, PAIRS, Q * Q))
    for pair in range(Q * Q):
        pick[0, pair, pair] = 1.0
    for q in range(Q):
        for p in range(q, Q):
            pick[1, sym_index(q, p), q * Q + p] += 0.5
            pick[1, sym_index(q, p), p * Q + q] += 0.5
    return (
        halves(z_basis.T),
        halves(z_basis),
        halves(basis),
        halves(basis.T),
        pick.astype(ml_dtypes.bfloat16),
    )


def split(value):
    high = value.astype(BF16)
    return high, (value - high.astype(F32)).astype(BF16)


def mm(a, b, dims=(((1,), (0,)), ((), ()))):
    return lax.dot_general(a, b, dims, preferred_element_type=F32)


def mm3(a, b, dims=(((1,), (0,)), ((), ()))):
    (ah, al), (bh, bl) = a, b
    return mm(ah, bh, dims) + (mm(al, bh, dims) + mm(ah, bl, dims))


def lanes_iota(rows):
    return lax.broadcasted_iota(jnp.int32, (rows, N), 1)


def turn(values, back):
    values = list(values)
    lane = lax.broadcasted_iota(jnp.int32, values[0].shape, values[0].ndim - 1)
    axis = values[0].ndim - 1
    for bit in (0, 1, 2):
        step = 1 << bit
        low = (lane & step) == 0
        for i in range(8):
            if i & step:
                continue
            j = i | step
            first, second = values[i], values[j]
            values[i] = jnp.where(low, first, pltpu.roll(second, step, axis))
            values[j] = jnp.where(low, pltpu.roll(first, N - step, axis), second)
    return values


def kernel(theta, phi, dphi, zf, zb, xf, xb, pick, u_out, stress_out, energy_out,
           s1, b1, p1, a1, spec, uspec, grad, v1, a2, w1, c1, partner, ktab, tabs, sums_a, sums_b, part,
           send_sem, recv1, recv2, recv3, recv4, sib_sem, sum_sem):
    gx = lax.axis_index("gx")
    gy = lax.axis_index("gy")
    core = lax.rem(gy, 2)
    plane = gx * GY + gy
    kz_low = plane // 2
    is_znyq = plane == 1
    kz = jnp.where(is_znyq, HALF, kz_low)
    sib = gy + 1 - 2 * core

    barrier = pltpu.get_barrier_semaphore()

    def hello_y(i, c):
        pl.semaphore_signal(barrier, inc=1, device_id=(gx, lax.rem(gy + i, GY)), device_id_type=MESH)
        return c

    def hello_x(i, c):
        pl.semaphore_signal(barrier, inc=1, device_id=(lax.rem(gx + i, GX), gy), device_id_type=MESH)
        return c

    lax.fori_loop(1, GY, hello_y, 0)
    lax.fori_loop(1, GX, hello_x, 0)

    zfh, zfl = zf[0], zf[1]
    for c in range(NC):
        block = theta[pl.ds(c * NQ, NQ)].reshape(NQ * 8 * 16, N)
        out = mm3(split(block), (zfh, zfl)).reshape(NQ, 8, 16, N)
        turned = turn([out[:, x] for x in range(8)], False)
        for g in range(GY):
            s1[g, pl.ds(c * NQ, NQ)] = turned[g]

    pl.semaphore_wait(barrier, GX + GY - 2)

    for c in range(NC):
        qs = pl.ds(c * NQ, NQ)

        def send1(i, k, qs=qs, c=c):
            to = lax.rem(gy + i, GY)
            pltpu.make_async_remote_copy(
                s1.at[to, qs], b1.at[qs, pl.ds(gy * 16, 16)], send_sem.at[0], recv1.at[c],
                device_id=(gx, to), device_id_type=MESH).start()
            return k

        lax.fori_loop(1, GY, send1, 0)
        b1[qs, pl.ds(gy * 16, 16)] = s1[gy, qs]

    phi_h, phi_l = split(phi[...])
    dphi_h, dphi_l = split(dphi[...])
    nt = (((1,), (1,)), ((), ()))
    table = (mm(pick[0], phi_h, nt) + mm(pick[0], phi_l, nt)) + (mm(pick[1], dphi_h, nt) + mm(pick[1], dphi_l, nt))
    tabs[0:PAIRS], tabs[PAIRS:2 * PAIRS] = split(table)
    tabs[2 * PAIRS:3 * PAIRS], tabs[3 * PAIRS:] = split(pltpu.roll(table, TABLE - 1, 1) - table)

    lane256 = lax.broadcasted_iota(jnp.int32, (1, 2 * N), 1)
    ky256 = jnp.where(lax.rem(lane256, N) == HALF, HALF, lane256 & (HALF - 1))
    second256 = lane256 // N

    def look_up(step, width):
        row = 2 * step
        first = jnp.where(row > HALF, row - HALF, row)
        near = first * first + kz * kz
        start = 0
        if width < TABLE:
            for t in range(1, (TABLE - width) // N + 1):
                start = start + jnp.minimum(near // math.ceil(t * t * 128.0 * 128.0 * 3 * 4096 / (1023.0 * 1023.0)), 1)
        base = pl.multiple_of(start * N, N)
        kx = row + second256
        kx = jnp.where(kx > HALF, kx - HALF, kx)
        square = kx * kx + ky256 * ky256 + kz * kz
        radial = jnp.sqrt(square.astype(F32)) * ((TABLE - 1) / (HALF * math.sqrt(3.0)))
        lower = jnp.clip(jnp.floor(radial), 0.0, TABLE - 2.0)
        fraction = radial - lower
        index = lower.astype(jnp.int32) - start * N
        points = lax.broadcasted_iota(jnp.int32, (width, 2 * N), 0)
        onehot = jnp.where(points == index, 1.0, 0.0).astype(BF16)
        out = mm(tabs[:, pl.ds(base, width)], onehot)
        value = (out[0:PAIRS] + out[PAIRS:2 * PAIRS]) + fraction * (out[2 * PAIRS:3 * PAIRS] + out[3 * PAIRS:])
        ktab[pl.ds(row, PAIRS, stride=KROWS), :] = value[:, 0:N]
        ktab[pl.ds(row + 1, PAIRS, stride=KROWS), :] = value[:, N:]

    def look_wide(step, k):
        look_up(step, TABLE)
        return k

    def look_narrow(step, k):
        look_up(step, 512)
        return k

    lax.fori_loop(0, 15, look_wide, 0)

    xfh, xfl = xf[0], xf[1]
    xbh, xbl = xb[0], xb[1]
    for c in range(NC):
        qs = pl.ds(c * NQ, NQ)
        got = b1.at[qs, pl.ds(0, 112)]
        pltpu.make_async_copy(got, got, recv1.at[c]).wait()
        for q in range(c * NQ, (c + 1) * NQ):
            p1[q] = mm3(split(b1[q].T), (xbh, xbl))

        def send2(i, k, qs=qs, c=c):
            to = lax.rem(gx + i, GX)
            pltpu.make_async_remote_copy(
                p1.at[qs, pl.ds(to * 8, 8)], a1.at[qs, pl.ds(gx * 8, 8)], send_sem.at[1], recv2.at[c],
                device_id=(to, gy), device_id_type=MESH).start()
            return k

        lax.fori_loop(1, GX, send2, 0)
        a1[qs, pl.ds(gx * 8, 8)] = p1[qs, pl.ds(gx * 8, 8)]
        first = 15 + 4 * c
        if c < NC - 1:
            lax.fori_loop(first, first + 4, look_narrow, 0)
        else:
            lax.fori_loop(first, 32, look_narrow, 0)
            lax.fori_loop(32, 36, look_wide, 0)

    for c in range(NC):
        qs = pl.ds(c * NQ, NQ)
        got = a1.at[qs, pl.ds(0, 120)]
        pltpu.make_async_copy(got, got, recv2.at[c]).wait()
        for q in range(c * NQ, (c + 1) * NQ):
            spec[q] = mm3((xfh, xfl), split(a1[q])).reshape(2, HALF, N)

    to_sibling = pltpu.make_async_remote_copy(
        spec.at[:, :, pl.ds((1 - core) * 32, 32)], partner, sib_sem.at[0], sib_sem.at[1],
        device_id=(gx, sib), device_id_type=MESH)
    to_sibling.start()

    def contract(tile, energy):
        parity = tile // 8
        place = pl.ds(pl.multiple_of(lax.rem(tile, 8) * 8, 8), 8)
        krow = jnp.where(tile == 8, HALF, lax.rem(tile, 8) * 8)
        s = [spec[q, parity, place] for q in range(Q)]
        for q in range(Q):
            acc = None
            for p in range(Q):
                term = ktab[pl.ds(pl.multiple_of((q * Q + p) * KROWS + krow, 8), 8), :] * s[p]
                acc = term if acc is None else acc + term
            uspec[q, parity, place] = acc
            energy = energy + acc * s[q]
        return energy

    zero = jnp.zeros((8, N), F32)
    energy = lax.fori_loop(0, 16, contract, zero)

    for c in range(NC):
        qs = pl.ds(c * NQ, NQ)
        for q in range(c * NQ, (c + 1) * NQ):
            v1[q] = mm3((xbh, xbl), split(uspec[q].reshape(N, N)))

        def send3(i, k, qs=qs, c=c):
            to = lax.rem(gx + i, GX)
            pltpu.make_async_remote_copy(
                v1.at[qs, pl.ds(to * 8, 8)], a2.at[qs, pl.ds(gx * 8, 8)], send_sem.at[2], recv3.at[c],
                device_id=(to, gy), device_id_type=MESH).start()
            return k

        lax.fori_loop(1, GX, send3, 0)
        a2[qs, pl.ds(gx * 8, 8)] = v1[qs, pl.ds(gx * 8, 8)]

    lane = lanes_iota(8)
    sub = lax.broadcasted_iota(jnp.int32, (8, N), 0)
    j = lane & (HALF - 1)
    ky_off = j.astype(F32)
    ky_full = jnp.where(lane == HALF, HALF, j).astype(F32)
    sy = lane // HALF
    ynyq = lane == HALF
    top = float(HALF * HALF)
    kz_f = kz.astype(F32)
    kz_off = kz_low.astype(F32)

    def moments(tile, sums):
        parity = tile // 8
        place = pl.ds(pl.multiple_of(lax.rem(tile, 8) * 8, 8), 8)
        krow = jnp.where(tile == 8, HALF, lax.rem(tile, 8) * 8)
        s = [spec[q, parity, place] for q in range(Q)]
        weight = zero
        cross = zero
        for q in range(Q):
            acc = None
            for p in range(Q):
                term = ktab[pl.ds(pl.multiple_of(sym_index(q, p) * KROWS + krow, 8), 8), :] * s[p]
                acc = term if acc is None else acc + term
            grad[q, parity, place] = acc
            weight = weight + acc * s[q]
            cross = cross + acc * pltpu.roll(spec[q, 1 - parity, place], HALF, 1)
        i = lax.rem(tile, 8) * 8 + sub
        kx_off = i.astype(F32)
        xnyq = (i == 0) & (parity == 1)
        kx_full = jnp.where(xnyq, top, kx_off * kx_off)
        xx, yy, zz, xy, xz, yz = sums
        xx = xx + weight * kx_full
        yy = yy + weight * (ky_full * ky_full)
        zz = zz + weight
        sign = jnp.where(sy == parity, -1.0, 1.0)
        xy = xy + cross * (sign * kx_off * ky_off) + jnp.where(xnyq & ynyq, weight * top, 0.0)
        xz = xz + jnp.where(xnyq & is_znyq, weight * top, 0.0)
        yz = yz + jnp.where(ynyq & is_znyq, weight * top, 0.0)
        return xx, yy, zz, xy, xz, yz

    xx, yy, zz, xy, xz, yz = lax.fori_loop(0, 16, moments, (zero,) * 6)

    to_sibling.wait()

    def mixed(step, sums):
        parity = step // 4
        here = lax.rem(step, 4) * 8
        mine = pl.ds(pl.multiple_of(core * 32 + here, 8), 8)
        theirs = pl.ds(pl.multiple_of(here, 8), 8)
        along_x = zero
        along_y = zero
        for q in range(Q):
            g = grad[q, parity, mine]
            along_x = along_x + g * partner[q, 1 - parity, theirs]
            along_y = along_y + g * pltpu.roll(partner[q, parity, theirs], HALF, 1)
        kx_off = (core * 32 + here + sub).astype(F32)
        xz, yz = sums
        xz = xz + along_x * (jnp.where(parity == core, -2.0, 2.0) * kz_off * kx_off)
        yz = yz + along_y * (jnp.where(sy == core, -2.0, 2.0) * kz_off * ky_off)
        return xz, yz

    xz, yz = lax.fori_loop(0, 8, mixed, (xz, yz))
    zz = zz * (kz_f * kz_f)
    part[...] = zero
    for row, total in enumerate((energy, xx, yy, zz, xy, xz, yz)):
        part[pl.ds(row, 1)] = jnp.sum(total, axis=0, keepdims=True)
    sums_a[gy] = part[...]

    def send_sum_y(i, k):
        to = lax.rem(gy + i, GY)
        pltpu.make_async_remote_copy(part, sums_a.at[gy], send_sem.at[4], sum_sem.at[0],
                                     device_id=(gx, to), device_id_type=MESH).start()
        return k

    lax.fori_loop(1, GY, send_sum_y, 0)

    for c in range(NC):
        qs = pl.ds(c * NQ, NQ)
        got = a2.at[qs, pl.ds(0, 120)]
        pltpu.make_async_copy(got, got, recv3.at[c]).wait()
        for q in range(c * NQ, (c + 1) * NQ):
            w1[q] = mm3((xbh, xbl), split(a2[q].T))

        def send4(i, k, qs=qs, c=c):
            to = lax.rem(gy + i, GY)
            pltpu.make_async_remote_copy(
                w1.at[qs, pl.ds(to * 16, 16)], c1.at[gy, qs], send_sem.at[3], recv4.at[c],
                device_id=(gx, to), device_id_type=MESH).start()
            return k

        lax.fori_loop(1, GY, send4, 0)
        c1[gy, qs] = w1[qs, pl.ds(gy * 16, 16)]

    got = sums_a.at[pl.ds(0, GY - 1)]
    pltpu.make_async_copy(got, got, sum_sem.at[0]).wait()
    total = sums_a[0]
    for i in range(1, GY):
        total = total + sums_a[i]
    sums_b[gx] = total

    def send_sum_x(i, k):
        to = lax.rem(gx + i, GX)
        pltpu.make_async_remote_copy(sums_b.at[gx], sums_b.at[gx], send_sem.at[5], sum_sem.at[1],
                                     device_id=(to, gy), device_id_type=MESH).start()
        return k

    lax.fori_loop(1, GX, send_sum_x, 0)

    zbh, zbl = zb[0], zb[1]
    for c in range(NC):
        qs = pl.ds(c * NQ, NQ)
        got = c1.at[pl.ds(0, GY - 1), qs]
        pltpu.make_async_copy(got, got, recv4.at[c]).wait()
        turned = turn([c1[g, qs] for g in range(GY)], True)
        for x in range(8):
            block = mm3(split(turned[x].reshape(NQ * 16, N)), (zbh, zbl))
            u_out[qs, x] = block.reshape(NQ, 16, N)

    got = sums_b.at[pl.ds(0, GX - 1)]
    pltpu.make_async_copy(got, got, sum_sem.at[1]).wait()
    total = sums_b[0]
    for i in range(1, GX):
        total = total + sums_b[i]
    cells = float(N) ** 3
    wave = (2.0 * math.pi / N) ** 2
    sums = jnp.sum(total, axis=1, keepdims=True)
    row = lax.broadcasted_iota(jnp.int32, (8, 1), 0)

    def pick_sum(r):
        return jnp.sum(jnp.where(row == r, sums, 0.0), axis=0, keepdims=True)

    energy_out[...] = pick_sum(0) * (0.5 / cells)
    r3 = lax.broadcasted_iota(jnp.int32, (3, 3), 0)
    c3 = lax.broadcasted_iota(jnp.int32, (3, 3), 1)
    stress = jnp.zeros((3, 3), F32)
    for r, (a, b) in enumerate(((0, 0), (1, 1), (2, 2), (0, 1), (0, 2), (1, 2))):
        here = ((r3 == a) & (c3 == b)) | ((r3 == b) & (c3 == a))
        stress = jnp.where(here, pick_sum(r + 1) * (-0.5 * wave / cells), stress)
    stress_out[...] = stress

    for slot, buffer in ((0, s1.at[pl.ds(0, GY - 1)]), (1, p1.at[:, pl.ds(0, 120)]), (2, v1.at[:, pl.ds(0, 120)]),
                         (3, w1.at[:, pl.ds(0, 112)]), (4, sums_a.at[pl.ds(0, GY - 1)]), (5, sums_b.at[pl.ds(0, GX - 1)])):
        pltpu.make_async_copy(buffer, buffer, send_sem.at[slot]).wait()


def shards(theta, phi, dphi):
    vmem = pl.BlockSpec(memory_space=pltpu.VMEM)
    cube = pltpu.VMEM((Q, N, N), F32)
    halves_cube = pltpu.VMEM((Q, 2, HALF, N), F32)
    small = pltpu.VMEM((GY, Q, 16, N), F32)
    u, stress, energy = pl.pallas_call(
        kernel,
        out_shape=(
            jax.ShapeDtypeStruct((Q, 8, 16, N), F32),
            jax.ShapeDtypeStruct((3, 3), F32),
            jax.ShapeDtypeStruct((1, 1), F32),
        ),
        in_specs=[vmem] * 8,
        out_specs=(vmem,) * 3,
        scratch_shapes=[
            small, cube, cube, cube, halves_cube, halves_cube, halves_cube, cube, cube, cube, small,
            pltpu.VMEM((Q, 2, 32, N), F32),
            pltpu.VMEM((PAIRS * KROWS, N), F32),
            pltpu.VMEM((4 * PAIRS, TABLE), BF16),
            pltpu.VMEM((GY, 8, N), F32),
            pltpu.VMEM((GX, 8, N), F32),
            pltpu.VMEM((8, N), F32),
            pltpu.SemaphoreType.DMA((6,)),
            pltpu.SemaphoreType.DMA((NC,)),
            pltpu.SemaphoreType.DMA((NC,)),
            pltpu.SemaphoreType.DMA((NC,)),
            pltpu.SemaphoreType.DMA((NC,)),
            pltpu.SemaphoreType.DMA((2,)),
            pltpu.SemaphoreType.DMA((2,)),
        ],
        compiler_params=pltpu.CompilerParams(
            collective_id=0, has_side_effects=True, vmem_limit_bytes=48 << 20),
    )(theta, phi, dphi, *(jnp.asarray(c) for c in constants()))
    return u, stress, energy.reshape(())


def solution(mesh):
    return jax.shard_map(
        shards,
        mesh=mesh,
        in_specs=(P(None, "gx", "gy", None), P(), P()),
        out_specs=(P(None, "gx", "gy", None), P(), P()),
        check_vma=False,
    )
```

profile of v0, /device:TPU:1, one launch (start us, length us, event | category | flops | bytes accessed | tf_op | source)
XLA Modules:
  0.0 53.7 jit_solution(1370447286629398656)
XLA Ops:
  0.6 0.0 copy-start.6
  0.6 0.0 copy-start.5
  0.7 1.3 %copy.11.phi = f32[1024,100]{1,0:T(8,128)S(1)} copy(f32[1024,100]{0,1:T(8,128)} %param.9) | data formatting | bytes 819200 | tf_op args[1]
  1.9 0.0 copy-done.6
  1.9 0.0 copy-start
  1.9 0.0 copy-start.1
  2.0 0.0 copy-start.2
  2.0 0.0 copy-start.3
  2.0 0.0 copy-start.4
  2.0 0.2 copy.12.dphi
  2.2 0.0 copy-done.5
  2.2 0.8 %copy-done = f32[10,8,16,128]{3,2,1,0:T(8,128)S(1)} copy-done((f32[10,8,16,128]{3,2,1,0:T(8,128)S(1)}, f32[10,8,16,128]{3,2,1,0:T(8,128)}, u32[]{:S(2)}) %copy-start) | copy-done | bytes 655384
  3.0 0.0 copy-done.1
  3.0 0.0 copy-done.2
  3.0 0.0 copy-done.3
  3.0 0.0 copy-done.4
  3.0 47.5 %shard_map.103 = (f32[10,8,16,128]{3,2,1,0:T(8,128)S(1)}, f32[3,3]{1,0:T(4,128)S(1)}, f32[1,1]{1,0:T(1,128)}) custom-call(f32[10,8,16,128]{3,2,1,0:T(8,128)S(1)} %copy-done, f32[1024,100]{1,0:T(8,128)S(1)} %copy.11.phi, f32[1024,100]{1,0:T(8,128)S(1)} %copy.12.dphi, bf16[2,128,128]{2,1,0:T(8,128)(2,1)S(1)} %copy-done.5, bf16[2,128,128]{2,1,0:T(8,128)(2,1)S(1)} %copy-done.4, ...), custom_call_target="tpu_custom_call" | custom-call | tf_op jit(solution)/shard_map/pallas_call | solution.py:414
  50.5 0.8 %copy.16 = f32[10,8,16,128]{3,2,1,0:T(8,128)} copy(f32[10,8,16,128]{3,2,1,0:T(8,128)S(1)} %get-tuple-element.12) | data formatting | bytes 1310720
  51.4 0.6 %copy.17 = f32[3,3]{1,0:T(4,128)} copy(f32[3,3]{1,0:T(4,128)S(1)} %get-tuple-element.13) | data formatting | bytes 72
Async XLA Ops:
  0.6 1.3 %copy-start.6 = (f32[1024,100]{0,1:T(8,128)S(1)}, f32[1024,100]{0,1:T(8,128)}, u32[]{:S(2)}) copy-start(f32[1024,100]{0,1:T(8,128)} %param.10) | copy-start | bytes 1228804
  0.6 1.6 %copy-start.5 = (bf16[2,128,128]{2,1,0:T(8,128)(2,1)S(1)}, bf16[2,128,128]{2,1,0:T(8,128)(2,1)}, u32[]{:S(2)}) copy-start(bf16[2,128,128]{2,1,0:T(8,128)(2,1)} %constant.10.clone.zf) | copy-start | bytes 196612
  1.9 1.1 %copy-start = (f32[10,8,16,128]{3,2,1,0:T(8,128)S(1)}, f32[10,8,16,128]{3,2,1,0:T(8,128)}, u32[]{:S(2)}) copy-start(f32[10,8,16,128]{3,2,1,0:T(8,128)} %theta.1) | copy-start | bytes 1966084
  1.9 1.1 %copy-start.1 = (bf16[2,160,100]{2,1,0:T(8,128)(2,1)S(1)}, bf16[2,160,100]{2,1,0:T(8,128)(2,1)}, u32[]{:S(2)}) copy-start(bf16[2,160,100]{2,1,0:T(8,128)(2,1)} %constant.14.clone.pick) | copy-start | bytes 192004
  2.0 1.1 %copy-start.2 = (bf16[2,128,128]{2,1,0:T(8,128)(2,1)S(1)}, bf16[2,128,128]{2,1,0:T(8,128)(2,1)}, u32[]{:S(2)}) copy-start(bf16[2,128,128]{2,1,0:T(8,128)(2,1)} %constant.13.clone.xb) | copy-start | bytes 196612
  2.0 1.1 %copy-start.3 = (bf16[2,128,128]{2,1,0:T(8,128)(2,1)S(1)}, bf16[2,128,128]{2,1,0:T(8,128)(2,1)}, u32[]{:S(2)}) copy-start(bf16[2,128,128]{2,1,0:T(8,128)(2,1)} %constant.12.clone.xf) | copy-start | bytes 196612
  2.0 1.1 %copy-start.4 = (bf16[2,128,128]{2,1,0:T(8,128)(2,1)S(1)}, bf16[2,128,128]{2,1,0:T(8,128)(2,1)}, u32[]{:S(2)}) copy-start(bf16[2,128,128]{2,1,0:T(8,128)(2,1)} %constant.11.clone.zb) | copy-start | bytes 196612
where the time goes:
time: 53.8 us; the launch traced here: 53.7 us
  Pallas kernels  47.5 us (88%)
  local copies, waits for them, and re-layouts  3.73 us (7%)
  between operations  2.42 us (4%)
    pallas_call x1, Pallas kernels, shards(): pl.pallas_call(kernel, out_shape=(jax.ShapeDtypeStruct((Q, 8, 16, N), F32...  47.5 us
    unnamed x18, local copies, waits for them, and re-layouts  3.73 us

commit v1 on v0

--- a/solution.py
+++ b/solution.py
@@ -17,9 +17,10 @@
 HALF = 64
 Q = 10
 GX = 16
+EARLY = 10
+FIRST = 64
 GY = 8
-NC = 5
-NQ = Q // NC
+ROWS = 10
 PAIRS = 160
 KROWS = 72
 TABLE = 1024
@@ -49,6 +50,8 @@
     basis = real_basis()
     order = np.array([(lane // 2) + HALF * (lane % 2) for lane in range(N)])
     z_basis = basis[order]
+    by_source = np.array([(i % GX) * 8 + i // GX for i in range(N)])
+    x_basis = basis[:, by_source]
     pick = np.zeros((2, PAIRS, Q * Q))
     for pair in range(Q * Q):
         pick[0, pair, pair] = 1.0
@@ -56,13 +59,8 @@
         for p in range(q, Q):
             pick[1, sym_index(q, p), q * Q + p] += 0.5
             pick[1, sym_index(q, p), p * Q + q] += 0.5
-    return (
-        halves(z_basis.T),
-        halves(z_basis),
-        halves(basis),
-        halves(basis.T),
-        pick.astype(ml_dtypes.bfloat16),
-    )
+    bases = np.stack([halves(b) for b in (z_basis, x_basis, x_basis.T, basis, basis.T)])
+    return bases, pick.astype(ml_dtypes.bfloat16)
 
 
 def split(value):
@@ -83,30 +81,36 @@
     return lax.broadcasted_iota(jnp.int32, (rows, N), 1)
 
 
-def turn(values, back):
+def exchange(values, lane_step):
     values = list(values)
-    lane = lax.broadcasted_iota(jnp.int32, values[0].shape, values[0].ndim - 1)
     axis = values[0].ndim - 1
-    for bit in (0, 1, 2):
-        step = 1 << bit
+    lane = lax.broadcasted_iota(jnp.int32, values[0].shape, axis)
+    bit = 1
+    while bit < len(values):
+        step = bit * lane_step
         low = (lane & step) == 0
-        for i in range(8):
-            if i & step:
+        for i in range(len(values)):
+            if i & bit:
                 continue
-            j = i | step
-            first, second = values[i], values[j]
+            first, second = values[i], values[i | bit]
             values[i] = jnp.where(low, first, pltpu.roll(second, step, axis))
-            values[j] = jnp.where(low, pltpu.roll(first, N - step, axis), second)
+            values[i | bit] = jnp.where(low, pltpu.roll(first, N - step, axis), second)
+        bit *= 2
     return values
 
 
-def kernel(theta, phi, dphi, zf, zb, xf, xb, pick, u_out, stress_out, energy_out,
-           s1, b1, p1, a1, spec, uspec, grad, v1, a2, w1, c1, partner, ktab, tabs, sums_a, sums_b, part,
-           send_sem, recv1, recv2, recv3, recv4, sib_sem, sum_sem):
+def kernel(theta_in, phi_in, dphi_in, bases_in, pick_in, u_out, stress_out, energy_out,
+           theta, phi, dphi, bases, pick, s1, r1, s2, r2, mid, spec, uspec, grad, partner, ktab, tabs, sums_a, sums_b, part,
+           send_sem, recv_sem, own_sem, sib_sem, sum_sem, in_sem):
+    inputs = [pltpu.make_async_copy(source, target, in_sem.at[i]) for i, (source, target) in enumerate(
+        ((theta_in, theta), (bases_in, bases), (phi_in, phi), (dphi_in, dphi), (pick_in, pick)))]
+    for copy in inputs:
+        copy.start()
     gx = lax.axis_index("gx")
     gy = lax.axis_index("gy")
     core = lax.rem(gy, 2)
     plane = gx * GY + gy
+    place_in_order = gy * GX + gx
     kz_low = plane // 2
     is_znyq = plane == 1
     kz = jnp.where(is_znyq, HALF, kz_low)
@@ -114,44 +118,29 @@
 
     barrier = pltpu.get_barrier_semaphore()
 
-    def hello_y(i, c):
-        pl.semaphore_signal(barrier, inc=1, device_id=(gx, lax.rem(gy + i, GY)), device_id_type=MESH)
+    def hello(i, c):
+        to = lax.rem(plane + i, N)
+        pl.semaphore_signal(barrier, inc=1, device_id=(to // GY, lax.rem(to, GY)), device_id_type=MESH)
         return c
 
-    def hello_x(i, c):
-        pl.semaphore_signal(barrier, inc=1, device_id=(lax.rem(gx + i, GX), gy), device_id_type=MESH)
-        return c
-
-    lax.fori_loop(1, GY, hello_y, 0)
-    lax.fori_loop(1, GX, hello_x, 0)
-
-    zfh, zfl = zf[0], zf[1]
-    for c in range(NC):
-        block = theta[pl.ds(c * NQ, NQ)].reshape(NQ * 8 * 16, N)
-        out = mm3(split(block), (zfh, zfl)).reshape(NQ, 8, 16, N)
-        turned = turn([out[:, x] for x in range(8)], False)
-        for g in range(GY):
-            s1[g, pl.ds(c * NQ, NQ)] = turned[g]
-
-    pl.semaphore_wait(barrier, GX + GY - 2)
-
-    for c in range(NC):
-        qs = pl.ds(c * NQ, NQ)
-
-        def send1(i, k, qs=qs, c=c):
-            to = lax.rem(gy + i, GY)
-            pltpu.make_async_remote_copy(
-                s1.at[to, qs], b1.at[qs, pl.ds(gy * 16, 16)], send_sem.at[0], recv1.at[c],
-                device_id=(gx, to), device_id_type=MESH).start()
-            return k
-
-        lax.fori_loop(1, GY, send1, 0)
-        b1[qs, pl.ds(gy * 16, 16)] = s1[gy, qs]
-
+    lax.fori_loop(1, N, hello, 0)
+
+    nt = (((1,), (1,)), ((), ()))
+    inputs[0].wait()
+    inputs[1].wait()
+    zbh, zbl = bases[0, 0], bases[0, 1]
+    for x in range(8):
+        block = theta[0:8, x].reshape(N, N)
+        s1[pl.ds(x, N, stride=ROWS), :] = mm3((zbh, zbl), split(block), nt)
+    for r in range(2):
+        block = jnp.concatenate([theta[8 + q, 2 * b + r] for b in range(4) for q in range(2)], axis=0)
+        s1[pl.ds(8 + r, N, stride=ROWS), :] = mm3((zbh, zbl), split(block), nt)
+
+    for copy in inputs[2:]:
+        copy.wait()
     phi_h, phi_l = split(phi[...])
     dphi_h, dphi_l = split(dphi[...])
-    nt = (((1,), (1,)), ((), ()))
-    table = (mm(pick[0], phi_h, nt) + mm(pick[0], phi_l, nt)) + (mm(pick[1], dphi_h, nt) + mm(pick[1], dphi_l, nt))
+    table = (mm(pick[0], phi_h) + mm(pick[0], phi_l)) + (mm(pick[1], dphi_h) + mm(pick[1], dphi_l))
     tabs[0:PAIRS], tabs[PAIRS:2 * PAIRS] = split(table)
     tabs[2 * PAIRS:3 * PAIRS], tabs[3 * PAIRS:] = split(pltpu.roll(table, TABLE - 1, 1) - table)
 
@@ -183,46 +172,59 @@
         ktab[pl.ds(row + 1, PAIRS, stride=KROWS), :] = value[:, N:]
 
     def look_wide(step, k):
-        look_up(step, TABLE)
+        look_up(step, 768)
         return k
 
     def look_narrow(step, k):
         look_up(step, 512)
         return k
 
-    lax.fori_loop(0, 15, look_wide, 0)
-
-    xfh, xfl = xf[0], xf[1]
-    xbh, xbl = xb[0], xb[1]
-    for c in range(NC):
-        qs = pl.ds(c * NQ, NQ)
-        got = b1.at[qs, pl.ds(0, 112)]
-        pltpu.make_async_copy(got, got, recv1.at[c]).wait()
-        for q in range(c * NQ, (c + 1) * NQ):
-            p1[q] = mm3(split(b1[q].T), (xbh, xbl))
-
-        def send2(i, k, qs=qs, c=c):
-            to = lax.rem(gx + i, GX)
-            pltpu.make_async_remote_copy(
-                p1.at[qs, pl.ds(to * 8, 8)], a1.at[qs, pl.ds(gx * 8, 8)], send_sem.at[1], recv2.at[c],
-                device_id=(to, gy), device_id_type=MESH).start()
-            return k
-
-        lax.fori_loop(1, GX, send2, 0)
-        a1[qs, pl.ds(gx * 8, 8)] = p1[qs, pl.ds(gx * 8, 8)]
-        first = 15 + 4 * c
-        if c < NC - 1:
-            lax.fori_loop(first, first + 4, look_narrow, 0)
-        else:
-            lax.fori_loop(first, 32, look_narrow, 0)
-            lax.fori_loop(32, 36, look_wide, 0)
-
-    for c in range(NC):
-        qs = pl.ds(c * NQ, NQ)
-        got = a1.at[qs, pl.ds(0, 120)]
-        pltpu.make_async_copy(got, got, recv2.at[c]).wait()
-        for q in range(c * NQ, (c + 1) * NQ):
-            spec[q] = mm3((xfh, xfl), split(a1[q])).reshape(2, HALF, N)
+    lax.fori_loop(0, EARLY, look_wide, 0)
+    pl.semaphore_wait(barrier, N - 1)
+
+    def send1(i, c):
+        to = lax.rem(plane + i, N)
+        pltpu.make_async_remote_copy(
+            s1.at[pl.ds(to * ROWS, ROWS)], r1.at[pl.ds(place_in_order * ROWS, ROWS)], send_sem.at[0], recv_sem.at[0],
+            device_id=(to // GY, lax.rem(to, GY)), device_id_type=MESH).start()
+        return c
+
+    lax.fori_loop(1, N, send1, 0)
+    own1 = pltpu.make_async_copy(
+        s1.at[pl.ds(plane * ROWS, ROWS)], r1.at[pl.ds(place_in_order * ROWS, ROWS)], own_sem.at[0])
+    own1.start()
+
+    lax.fori_loop(EARLY, 15, look_wide, 0)
+    lax.fori_loop(15, 32, look_narrow, 0)
+    look_up(32, TABLE)
+    lax.fori_loop(33, 36, look_wide, 0)
+
+    xfh, xfl = bases[1, 0], bases[1, 1]
+    all_but_one = pl.ds(0, (N - 1) * ROWS)
+    got = r1.at[all_but_one]
+    pltpu.make_async_copy(got, got, recv_sem.at[0]).wait()
+    own1.wait()
+    for g in range(GY):
+        block = jnp.concatenate([r1[pl.ds(g * GX * ROWS + x, GX, stride=ROWS), :] for x in range(8)], axis=0)
+        mid[g] = mm3((xfh, xfl), split(block))
+    for h in range(2):
+        ends = [jnp.concatenate([r1[pl.ds((2 * a + h) * GX * ROWS + 8 + r, GX, stride=ROWS), :] for r in range(2)], axis=0)
+                for a in range(4)]
+        mid[8 + h] = mm3((xfh, xfl), split(jnp.concatenate(exchange(ends, 32), axis=0)))
+
+    def regroup(tile, c):
+        place = pl.ds(pl.multiple_of(tile * 32, 32), 32)
+        main = exchange([mid[i, place] for i in range(8)], 16)
+        ends = exchange([mid[i, place] for i in (8, 9)], 16)
+        for i, value in enumerate(main + ends):
+            mid[i, place] = value
+        return c
+
+    lax.fori_loop(0, 4, regroup, 0)
+
+    ybh, ybl = bases[4, 0], bases[4, 1]
+    for q in range(Q):
+        spec[q] = mm3(split(mid[q]), (ybh, ybl)).reshape(2, HALF, N)
 
     to_sibling = pltpu.make_async_remote_copy(
         spec.at[:, :, pl.ds((1 - core) * 32, 32)], partner, sib_sem.at[0], sib_sem.at[1],
@@ -246,20 +248,35 @@
     zero = jnp.zeros((8, N), F32)
     energy = lax.fori_loop(0, 16, contract, zero)
 
-    for c in range(NC):
-        qs = pl.ds(c * NQ, NQ)
-        for q in range(c * NQ, (c + 1) * NQ):
-            v1[q] = mm3((xbh, xbl), split(uspec[q].reshape(N, N)))
-
-        def send3(i, k, qs=qs, c=c):
-            to = lax.rem(gx + i, GX)
-            pltpu.make_async_remote_copy(
-                v1.at[qs, pl.ds(to * 8, 8)], a2.at[qs, pl.ds(gx * 8, 8)], send_sem.at[2], recv3.at[c],
-                device_id=(to, gy), device_id_type=MESH).start()
-            return k
-
-        lax.fori_loop(1, GX, send3, 0)
-        a2[qs, pl.ds(gx * 8, 8)] = v1[qs, pl.ds(gx * 8, 8)]
+    yfh, yfl = bases[3, 0], bases[3, 1]
+    for q in range(Q):
+        mid[q] = mm3(split(uspec[q].reshape(N, N)), (yfh, yfl))
+    lax.fori_loop(0, 4, regroup, 0)
+
+    xbh, xbl = bases[2, 0], bases[2, 1]
+    for g in range(GY):
+        block = mm3((xbh, xbl), split(mid[g]))
+        for x in range(8):
+            s2[pl.ds(g * GX * ROWS + x, GX, stride=ROWS), :] = block[x * GX:(x + 1) * GX]
+    for h in range(2):
+        block = mm3((xbh, xbl), split(mid[8 + h]))
+        ends = exchange([block[b * 32:(b + 1) * 32] for b in range(4)], 32)
+        for a in range(4):
+            for r in range(2):
+                s2[pl.ds((2 * a + h) * GX * ROWS + 8 + r, GX, stride=ROWS), :] = ends[a][r * GX:(r + 1) * GX]
+
+    def send2(i, c):
+        to = lax.rem(plane + i, N)
+        to_x, to_y = to // GY, lax.rem(to, GY)
+        pltpu.make_async_remote_copy(
+            s2.at[pl.ds((to_y * GX + to_x) * ROWS, ROWS)], r2.at[pl.ds(plane * ROWS, ROWS)], send_sem.at[1], recv_sem.at[1],
+            device_id=(to_x, to_y), device_id_type=MESH).start()
+        return c
+
+    lax.fori_loop(1, FIRST, send2, 0)
+    own2 = pltpu.make_async_copy(
+        s2.at[pl.ds(place_in_order * ROWS, ROWS)], r2.at[pl.ds(plane * ROWS, ROWS)], own_sem.at[1])
+    own2.start()
 
     lane = lanes_iota(8)
     sub = lax.broadcasted_iota(jnp.int32, (8, N), 0)
@@ -331,28 +348,12 @@
 
     def send_sum_y(i, k):
         to = lax.rem(gy + i, GY)
-        pltpu.make_async_remote_copy(part, sums_a.at[gy], send_sem.at[4], sum_sem.at[0],
+        pltpu.make_async_remote_copy(part, sums_a.at[gy], send_sem.at[2], sum_sem.at[0],
                                      device_id=(gx, to), device_id_type=MESH).start()
         return k
 
     lax.fori_loop(1, GY, send_sum_y, 0)
-
-    for c in range(NC):
-        qs = pl.ds(c * NQ, NQ)
-        got = a2.at[qs, pl.ds(0, 120)]
-        pltpu.make_async_copy(got, got, recv3.at[c]).wait()
-        for q in range(c * NQ, (c + 1) * NQ):
-            w1[q] = mm3((xbh, xbl), split(a2[q].T))
-
-        def send4(i, k, qs=qs, c=c):
-            to = lax.rem(gy + i, GY)
-            pltpu.make_async_remote_copy(
-                w1.at[qs, pl.ds(to * 16, 16)], c1.at[gy, qs], send_sem.at[3], recv4.at[c],
-                device_id=(gx, to), device_id_type=MESH).start()
-            return k
-
-        lax.fori_loop(1, GY, send4, 0)
-        c1[gy, qs] = w1[qs, pl.ds(gy * 16, 16)]
+    lax.fori_loop(FIRST, N, send2, 0)
 
     got = sums_a.at[pl.ds(0, GY - 1)]
     pltpu.make_async_copy(got, got, sum_sem.at[0]).wait()
@@ -363,21 +364,11 @@
 
     def send_sum_x(i, k):
         to = lax.rem(gx + i, GX)
-        pltpu.make_async_remote_copy(sums_b.at[gx], sums_b.at[gx], send_sem.at[5], sum_sem.at[1],
+        pltpu.make_async_remote_copy(sums_b.at[gx], sums_b.at[gx], send_sem.at[3], sum_sem.at[1],
                                      device_id=(to, gy), device_id_type=MESH).start()
         return k
 
     lax.fori_loop(1, GX, send_sum_x, 0)
-
-    zbh, zbl = zb[0], zb[1]
-    for c in range(NC):
-        qs = pl.ds(c * NQ, NQ)
-        got = c1.at[pl.ds(0, GY - 1), qs]
-        pltpu.make_async_copy(got, got, recv4.at[c]).wait()
-        turned = turn([c1[g, qs] for g in range(GY)], True)
-        for x in range(8):
-            block = mm3(split(turned[x].reshape(NQ * 16, N)), (zbh, zbl))
-            u_out[qs, x] = block.reshape(NQ, 16, N)
 
     got = sums_b.at[pl.ds(0, GX - 1)]
     pltpu.make_async_copy(got, got, sum_sem.at[1]).wait()
@@ -401,8 +392,21 @@
         stress = jnp.where(here, pick_sum(r + 1) * (-0.5 * wave / cells), stress)
     stress_out[...] = stress
 
-    for slot, buffer in ((0, s1.at[pl.ds(0, GY - 1)]), (1, p1.at[:, pl.ds(0, 120)]), (2, v1.at[:, pl.ds(0, 120)]),
-                         (3, w1.at[:, pl.ds(0, 112)]), (4, sums_a.at[pl.ds(0, GY - 1)]), (5, sums_b.at[pl.ds(0, GX - 1)])):
+    got = r2.at[all_but_one]
+    pltpu.make_async_copy(got, got, recv_sem.at[1]).wait()
+    own2.wait()
+    for x in range(8):
+        block = r2[pl.ds(x, N, stride=ROWS), :].T
+        u_out[0:8, x] = mm3(split(block), (zbh, zbl)).reshape(8, 16, N)
+    for r in range(2):
+        block = r2[pl.ds(8 + r, N, stride=ROWS), :].T
+        out = mm3(split(block), (zbh, zbl)).reshape(4, 2, 16, N)
+        for b in range(4):
+            for q in range(2):
+                u_out[8 + q, 2 * b + r] = out[b, q]
+
+    for slot, buffer in ((0, s1.at[all_but_one]), (1, s2.at[all_but_one]),
+                         (2, sums_a.at[pl.ds(0, GY - 1)]), (3, sums_b.at[pl.ds(0, GX - 1)])):
         pltpu.make_async_copy(buffer, buffer, send_sem.at[slot]).wait()
 
 
@@ -410,7 +414,7 @@
     vmem = pl.BlockSpec(memory_space=pltpu.VMEM)
     cube = pltpu.VMEM((Q, N, N), F32)
     halves_cube = pltpu.VMEM((Q, 2, HALF, N), F32)
-    small = pltpu.VMEM((GY, Q, 16, N), F32)
+    rows = pltpu.VMEM((N * ROWS, N), F32)
     u, stress, energy = pl.pallas_call(
         kernel,
         out_shape=(
@@ -418,27 +422,31 @@
             jax.ShapeDtypeStruct((3, 3), F32),
             jax.ShapeDtypeStruct((1, 1), F32),
         ),
-        in_specs=[vmem] * 8,
+        in_specs=[pl.BlockSpec(memory_space=pl.ANY)] * 5,
         out_specs=(vmem,) * 3,
         scratch_shapes=[
-            small, cube, cube, cube, halves_cube, halves_cube, halves_cube, cube, cube, cube, small,
+            pltpu.VMEM((Q, 8, 16, N), F32),
+            pltpu.VMEM((Q * Q, TABLE), F32),
+            pltpu.VMEM((Q * Q, TABLE), F32),
+            pltpu.VMEM((5, 2, N, N), BF16),
+            pltpu.VMEM((2, PAIRS, Q * Q), BF16),
+            rows, rows, rows, rows, cube, halves_cube, halves_cube, halves_cube,
             pltpu.VMEM((Q, 2, 32, N), F32),
             pltpu.VMEM((PAIRS * KROWS, N), F32),
             pltpu.VMEM((4 * PAIRS, TABLE), BF16),
             pltpu.VMEM((GY, 8, N), F32),
             pltpu.VMEM((GX, 8, N), F32),
             pltpu.VMEM((8, N), F32),
-            pltpu.SemaphoreType.DMA((6,)),
-            pltpu.SemaphoreType.DMA((NC,)),
-            pltpu.SemaphoreType.DMA((NC,)),
-            pltpu.SemaphoreType.DMA((NC,)),
-            pltpu.SemaphoreType.DMA((NC,)),
+            pltpu.SemaphoreType.DMA((4,)),
             pltpu.SemaphoreType.DMA((2,)),
             pltpu.SemaphoreType.DMA((2,)),
+            pltpu.SemaphoreType.DMA((2,)),
+            pltpu.SemaphoreType.DMA((2,)),
+            pltpu.SemaphoreType.DMA((5,)),
         ],
         compiler_params=pltpu.CompilerParams(
-            collective_id=0, has_side_effects=True, vmem_limit_bytes=48 << 20),
-    )(theta, phi, dphi, *(jnp.asarray(c) for c in constants()))
+            collective_id=0, has_side_effects=True, vmem_limit_bytes=56 << 20),
+    )(theta, phi.T, dphi.T, *(jnp.asarray(c) for c in constants()))
     return u, stress, energy.reshape(())
 
 

time: 53.8 us -> 51.1 us (0.950)
  Pallas kernels: 47.5 us -> 46 us
  local copies, waits for them, and re-layouts: 3.73 us -> 2.55 us
    pallas_call x1, Pallas kernels: 47.5 us -> 46 us  [shards(): pl.pallas_call(kernel, out_shape=(jax.ShapeDtypeStruct((Q, 8, 16, N), F32...]
    unnamed x18 -> x4, local copies, waits for them, and re-layouts: 3.73 us -> 2.55 us
where the time goes in v1:
time: 51.1 us; the launch traced here: 51 us
  Pallas kernels  46 us (90%)
  local copies, waits for them, and re-layouts  2.55 us (5%)
  between operations  2.35 us (5%)
    pallas_call x1, Pallas kernels, shards(): pl.pallas_call(kernel, out_shape=(jax.ShapeDtypeStruct((Q, 8, 16, N), F32...  46 us
    unnamed x4, local copies, waits for them, and re-layouts  2.55 us

profile of v1, /device:TPU:1, one launch (start us, length us, event | category | flops | bytes accessed | tf_op | source)
XLA Modules:
  0.0 51.0 jit_solution(11684649812139621689)
XLA Ops:
  0.6 46.0 %shard_map.76 = (f32[10,8,16,128]{3,2,1,0:T(8,128)}, f32[3,3]{1,0:T(4,128)}, f32[1,1]{1,0:T(1,128)}) custom-call(f32[10,8,16,128]{3,2,1,0:T(8,128)} %theta_in.1, f32[100,1024]{1,0:T(8,128)} %bitcast.3, f32[100,1024]{1,0:T(8,128)} %bitcast.4, bf16[5,2,128,128]{3,2,1,0:T(8,128)(2,1)} %constant.4.clone.bases_in, bf16[2,160,100]{2,1,0:T(8,128)(2,1)} %constant.5.clone.pick_in), custom_call_target="tpu_custom_call" | custom-call | tf_op jit(solution)/shard_map/pallas_call | solution.py:418
  46.7 0.0 copy-start
  46.7 2.0 %copy.11 = f32[10,8,16,128]{3,2,1,0:T(8,128)} copy(f32[10,8,16,128]{3,2,1,0:T(8,128)} %get-tuple-element.12) | data formatting | bytes 1310720
  48.7 0.0 copy-done
  48.7 0.6 %copy.12 = f32[3,3]{1,0:T(4,128)} copy(f32[3,3]{1,0:T(4,128)S(1)} %copy-done) | data formatting | bytes 72
Async XLA Ops:
  46.7 2.0 %copy-start = (f32[3,3]{1,0:T(4,128)S(1)}, f32[3,3]{1,0:T(4,128)}, u32[]{:S(2)}) copy-start(f32[3,3]{1,0:T(4,128)} %get-tuple-element.13) | copy-start | bytes 112

commit v2 on v1

--- a/solution.py
+++ b/solution.py
@@ -17,12 +17,15 @@
 HALF = 64
 Q = 10
 GX = 16
-EARLY = 10
-FIRST = 64
+REGROUP = 128
+FIRST, SECOND = 64, 96
 GY = 8
 ROWS = 10
-PAIRS = 160
-KROWS = 72
+VALUES = 104
+SLOPES = 56
+PAIRS = Q * Q + SLOPES
+GROUPS = 9
+SPLIT = 4
 TABLE = 1024
 
 
@@ -52,13 +55,11 @@
     z_basis = basis[order]
     by_source = np.array([(i % GX) * 8 + i // GX for i in range(N)])
     x_basis = basis[:, by_source]
-    pick = np.zeros((2, PAIRS, Q * Q))
-    for pair in range(Q * Q):
-        pick[0, pair, pair] = 1.0
+    pick = np.zeros((SLOPES, Q * Q))
     for q in range(Q):
         for p in range(q, Q):
-            pick[1, sym_index(q, p), q * Q + p] += 0.5
-            pick[1, sym_index(q, p), p * Q + q] += 0.5
+            pick[sym_index(q, p) - Q * Q, q * Q + p] += 0.5
+            pick[sym_index(q, p) - Q * Q, p * Q + q] += 0.5
     bases = np.stack([halves(b) for b in (z_basis, x_basis, x_basis.T, basis, basis.T)])
     return bases, pick.astype(ml_dtypes.bfloat16)
 
@@ -99,9 +100,9 @@
     return values
 
 
-def kernel(theta_in, phi_in, dphi_in, bases_in, pick_in, u_out, stress_out, energy_out,
-           theta, phi, dphi, bases, pick, s1, r1, s2, r2, mid, spec, uspec, grad, partner, ktab, tabs, sums_a, sums_b, part,
-           send_sem, recv_sem, own_sem, sib_sem, sum_sem, in_sem):
+def kernel(theta_in, phi_in, dphi_in, bases_in, pick_in, r2, total_out,
+           theta, phi, dphi, bases, pick, s1, r1, s2, mid, spec, uspec, grad, partner, ktab, tabs, sums_a, sums_b, part,
+           send_sem, recv_sem, own_sem, sib_sem, sum_sem, in_sem, tab_sem):
     inputs = [pltpu.make_async_copy(source, target, in_sem.at[i]) for i, (source, target) in enumerate(
         ((theta_in, theta), (bases_in, bases), (phi_in, phi), (dphi_in, dphi), (pick_in, pick)))]
     for copy in inputs:
@@ -138,11 +139,19 @@
 
     for copy in inputs[2:]:
         copy.wait()
-    phi_h, phi_l = split(phi[...])
-    dphi_h, dphi_l = split(dphi[...])
-    table = (mm(pick[0], phi_h) + mm(pick[0], phi_l)) + (mm(pick[1], dphi_h) + mm(pick[1], dphi_l))
-    tabs[0:PAIRS], tabs[PAIRS:2 * PAIRS] = split(table)
-    tabs[2 * PAIRS:3 * PAIRS], tabs[3 * PAIRS:] = split(pltpu.roll(table, TABLE - 1, 1) - table)
+
+    def halves_of(table, first):
+        difference = pltpu.roll(table, TABLE - 1, 1) - table
+        parts = []
+        for value in (table, difference):
+            high = value.astype(BF16).astype(F32)
+            parts += [high, value - high]
+        tabs[first:first + 4 * table.shape[0]] = jnp.concatenate(parts, axis=0).astype(BF16)
+
+    def prepare():
+        halves_of(jnp.concatenate([phi[...], jnp.zeros((VALUES - Q * Q, TABLE), F32)], axis=0), 0)
+        dphi_h, dphi_l = split(dphi[...])
+        halves_of(mm(pick[...], dphi_h) + mm(pick[...], dphi_l), 4 * VALUES)
 
     lane256 = lax.broadcasted_iota(jnp.int32, (1, 2 * N), 1)
     ky256 = jnp.where(lax.rem(lane256, N) == HALF, HALF, lane256 & (HALF - 1))
@@ -152,34 +161,67 @@
         row = 2 * step
         first = jnp.where(row > HALF, row - HALF, row)
         near = first * first + kz * kz
-        start = 0
+        first_tile = 0
         if width < TABLE:
             for t in range(1, (TABLE - width) // N + 1):
-                start = start + jnp.minimum(near // math.ceil(t * t * 128.0 * 128.0 * 3 * 4096 / (1023.0 * 1023.0)), 1)
-        base = pl.multiple_of(start * N, N)
+                first_tile = first_tile + jnp.minimum(near // math.ceil(t * t * 128.0 * 128.0 * 3 * 4096 / (1023.0 * 1023.0)), 1)
+        base = pl.multiple_of(first_tile * N, N)
         kx = row + second256
         kx = jnp.where(kx > HALF, kx - HALF, kx)
         square = kx * kx + ky256 * ky256 + kz * kz
         radial = jnp.sqrt(square.astype(F32)) * ((TABLE - 1) / (HALF * math.sqrt(3.0)))
         lower = jnp.clip(jnp.floor(radial), 0.0, TABLE - 2.0)
         fraction = radial - lower
-        index = lower.astype(jnp.int32) - start * N
+        index = lower.astype(jnp.int32) - first_tile * N
         points = lax.broadcasted_iota(jnp.int32, (width, 2 * N), 0)
         onehot = jnp.where(points == index, 1.0, 0.0).astype(BF16)
         out = mm(tabs[:, pl.ds(base, width)], onehot)
-        value = (out[0:PAIRS] + out[PAIRS:2 * PAIRS]) + fraction * (out[2 * PAIRS:3 * PAIRS] + out[3 * PAIRS:])
-        ktab[pl.ds(row, PAIRS, stride=KROWS), :] = value[:, 0:N]
-        ktab[pl.ds(row + 1, PAIRS, stride=KROWS), :] = value[:, N:]
-
-    def look_wide(step, k):
+        for first, count, pair in ((0, VALUES, 0), (4 * VALUES, SLOPES, Q * Q)):
+            part = [out[first + i * count:first + (i + 1) * count] for i in range(4)]
+            value = (part[0] + part[1]) + fraction * (part[2] + part[3])
+            start = (row // 8 * PAIRS + pair) * 8 + row % 8
+            ktab[pl.ds(start, count, stride=8), :] = value[:, 0:N]
+            ktab[pl.ds(start + 1, count, stride=8), :] = value[:, N:]
+
+    def wide(step, k):
         look_up(step, 768)
         return k
 
-    def look_narrow(step, k):
+    def narrow(step, k):
         look_up(step, 512)
         return k
 
-    lax.fori_loop(0, EARLY, look_wide, 0)
+    def last(step, k):
+        look_up(step, TABLE)
+        return k
+
+    def piece(group, slope):
+        return ktab.at[pl.ds((group * PAIRS + slope * Q * Q) * 8, (SLOPES if slope else Q * Q) * 8)]
+
+    def share(group, slope):
+        mine = piece(group, slope)
+        return pltpu.make_async_remote_copy(mine, mine, tab_sem.at[0, slope, group], tab_sem.at[1, slope, group],
+                                            device_id=(gx, sib), device_id_type=MESH)
+
+    owned = (range(SPLIT), range(SPLIT, GROUPS))
+
+    def look_group(group):
+        for first, until, body in ((0, 15, wide), (15, 32, narrow), (32, 33, last), (33, 36, wide)):
+            first, until = max(first, group * 4), min(until, group * 4 + 4)
+            if first < until:
+                lax.fori_loop(first, until, body, 0)
+
+    shares = plane > 1
+
+    @pl.when(plane <= 1)
+    def _():
+        prepare()
+        for owner in (0, 1):
+            @pl.when(core == owner)
+            def _(owner=owner):
+                for group in owned[1 - owner]:
+                    look_group(group)
+
     pl.semaphore_wait(barrier, N - 1)
 
     def send1(i, c):
@@ -194,10 +236,26 @@
         s1.at[pl.ds(plane * ROWS, ROWS)], r1.at[pl.ds(place_in_order * ROWS, ROWS)], own_sem.at[0])
     own1.start()
 
-    lax.fori_loop(EARLY, 15, look_wide, 0)
-    lax.fori_loop(15, 32, look_narrow, 0)
-    look_up(32, TABLE)
-    lax.fori_loop(33, 36, look_wide, 0)
+    @pl.when(shares)
+    def _():
+        prepare()
+
+    for owner in (0, 1):
+        @pl.when(core == owner)
+        def _(owner=owner):
+            for group in owned[owner]:
+                look_group(group)
+
+                @pl.when(shares)
+                def _(group=group):
+                    share(group, 0).start()
+                    share(group, 1).start()
+
+            @pl.when(shares)
+            def _():
+                for group in owned[1 - owner]:
+                    theirs = piece(group, 0)
+                    pltpu.make_async_copy(theirs, theirs, tab_sem.at[1, 0, group]).wait()
 
     xfh, xfl = bases[1, 0], bases[1, 1]
     all_but_one = pl.ds(0, (N - 1) * ROWS)
@@ -213,14 +271,14 @@
         mid[8 + h] = mm3((xfh, xfl), split(jnp.concatenate(exchange(ends, 32), axis=0)))
 
     def regroup(tile, c):
-        place = pl.ds(pl.multiple_of(tile * 32, 32), 32)
+        place = pl.ds(pl.multiple_of(tile * REGROUP, REGROUP), REGROUP)
         main = exchange([mid[i, place] for i in range(8)], 16)
         ends = exchange([mid[i, place] for i in (8, 9)], 16)
         for i, value in enumerate(main + ends):
             mid[i, place] = value
         return c
 
-    lax.fori_loop(0, 4, regroup, 0)
+    lax.fori_loop(0, N // REGROUP, regroup, 0)
 
     ybh, ybl = bases[4, 0], bases[4, 1]
     for q in range(Q):
@@ -234,12 +292,12 @@
     def contract(tile, energy):
         parity = tile // 8
         place = pl.ds(pl.multiple_of(lax.rem(tile, 8) * 8, 8), 8)
-        krow = jnp.where(tile == 8, HALF, lax.rem(tile, 8) * 8)
+        group = jnp.where(tile == 8, 8, lax.rem(tile, 8))
         s = [spec[q, parity, place] for q in range(Q)]
         for q in range(Q):
             acc = None
             for p in range(Q):
-                term = ktab[pl.ds(pl.multiple_of((q * Q + p) * KROWS + krow, 8), 8), :] * s[p]
+                term = ktab[pl.ds(pl.multiple_of((group * PAIRS + q * Q + p) * 8, 8), 8), :] * s[p]
                 acc = term if acc is None else acc + term
             uspec[q, parity, place] = acc
             energy = energy + acc * s[q]
@@ -251,7 +309,7 @@
     yfh, yfl = bases[3, 0], bases[3, 1]
     for q in range(Q):
         mid[q] = mm3(split(uspec[q].reshape(N, N)), (yfh, yfl))
-    lax.fori_loop(0, 4, regroup, 0)
+    lax.fori_loop(0, N // REGROUP, regroup, 0)
 
     xbh, xbl = bases[2, 0], bases[2, 1]
     for g in range(GY):
@@ -278,6 +336,16 @@
         s2.at[pl.ds(place_in_order * ROWS, ROWS)], r2.at[pl.ds(plane * ROWS, ROWS)], own_sem.at[1])
     own2.start()
 
+    for owner in (0, 1):
+        @pl.when(shares & (core == owner))
+        def _(owner=owner):
+            for group in owned[1 - owner]:
+                theirs = piece(group, 1)
+                pltpu.make_async_copy(theirs, theirs, tab_sem.at[1, 1, group]).wait()
+            for group in owned[owner]:
+                share(group, 0).wait_send()
+                share(group, 1).wait_send()
+
     lane = lanes_iota(8)
     sub = lax.broadcasted_iota(jnp.int32, (8, N), 0)
     j = lane & (HALF - 1)
@@ -292,14 +360,14 @@
     def moments(tile, sums):
         parity = tile // 8
         place = pl.ds(pl.multiple_of(lax.rem(tile, 8) * 8, 8), 8)
-        krow = jnp.where(tile == 8, HALF, lax.rem(tile, 8) * 8)
+        group = jnp.where(tile == 8, 8, lax.rem(tile, 8))
         s = [spec[q, parity, place] for q in range(Q)]
         weight = zero
         cross = zero
         for q in range(Q):
             acc = None
             for p in range(Q):
-                term = ktab[pl.ds(pl.multiple_of(sym_index(q, p) * KROWS + krow, 8), 8), :] * s[p]
+                term = ktab[pl.ds(pl.multiple_of((group * PAIRS + sym_index(q, p)) * 8, 8), 8), :] * s[p]
                 acc = term if acc is None else acc + term
             grad[q, parity, place] = acc
             weight = weight + acc * s[q]
@@ -353,7 +421,7 @@
         return k
 
     lax.fori_loop(1, GY, send_sum_y, 0)
-    lax.fori_loop(FIRST, N, send2, 0)
+    lax.fori_loop(FIRST, SECOND, send2, 0)
 
     got = sums_a.at[pl.ds(0, GY - 1)]
     pltpu.make_async_copy(got, got, sum_sem.at[0]).wait()
@@ -369,15 +437,48 @@
         return k
 
     lax.fori_loop(1, GX, send_sum_x, 0)
+    lax.fori_loop(SECOND, N, send2, 0)
 
     got = sums_b.at[pl.ds(0, GX - 1)]
     pltpu.make_async_copy(got, got, sum_sem.at[1]).wait()
     total = sums_b[0]
     for i in range(1, GX):
         total = total + sums_b[i]
+    total_out[...] = total
+
+    got = r2.at[all_but_one]
+    pltpu.make_async_copy(got, got, recv_sem.at[1]).wait()
+    own2.wait()
+
+    for slot, buffer in ((0, s1.at[all_but_one]), (1, s2.at[all_but_one]),
+                         (2, sums_a.at[pl.ds(0, GY - 1)]), (3, sums_b.at[pl.ds(0, GX - 1)])):
+        pltpu.make_async_copy(buffer, buffer, send_sem.at[slot]).wait()
+
+
+def finish(received, total_in, bases_in, u_out, stress_out, energy_out, rows_in, total, bases, u, in_sem, out_sem):
+    inputs = [pltpu.make_async_copy(source, target, in_sem.at[i]) for i, (source, target) in enumerate(
+        ((received, rows_in), (bases_in.at[0], bases), (total_in, total)))]
+    for copy in inputs:
+        copy.start()
+    for copy in inputs:
+        copy.wait()
+    zbh, zbl = bases[0], bases[1]
+    for r in range(2):
+        block = rows_in[pl.ds(8 + r, N, stride=ROWS), :].T
+        out = mm3(split(block), (zbh, zbl)).reshape(4, 2, 16, N)
+        for b in range(4):
+            for q in range(2):
+                u[2 * b + r, 8 + q] = out[b, q]
+    copies = []
+    for x in range(8):
+        block = rows_in[pl.ds(x, N, stride=ROWS), :].T
+        u[x, 0:8] = mm3(split(block), (zbh, zbl)).reshape(8, 16, N)
+        copies.append(pltpu.make_async_copy(u.at[x], u_out.at[:, x], out_sem.at[x]))
+        copies[-1].start()
+
     cells = float(N) ** 3
     wave = (2.0 * math.pi / N) ** 2
-    sums = jnp.sum(total, axis=1, keepdims=True)
+    sums = jnp.sum(total[...], axis=1, keepdims=True)
     row = lax.broadcasted_iota(jnp.int32, (8, 1), 0)
 
     def pick_sum(r):
@@ -391,49 +492,34 @@
         here = ((r3 == a) & (c3 == b)) | ((r3 == b) & (c3 == a))
         stress = jnp.where(here, pick_sum(r + 1) * (-0.5 * wave / cells), stress)
     stress_out[...] = stress
-
-    got = r2.at[all_but_one]
-    pltpu.make_async_copy(got, got, recv_sem.at[1]).wait()
-    own2.wait()
-    for x in range(8):
-        block = r2[pl.ds(x, N, stride=ROWS), :].T
-        u_out[0:8, x] = mm3(split(block), (zbh, zbl)).reshape(8, 16, N)
-    for r in range(2):
-        block = r2[pl.ds(8 + r, N, stride=ROWS), :].T
-        out = mm3(split(block), (zbh, zbl)).reshape(4, 2, 16, N)
-        for b in range(4):
-            for q in range(2):
-                u_out[8 + q, 2 * b + r] = out[b, q]
-
-    for slot, buffer in ((0, s1.at[all_but_one]), (1, s2.at[all_but_one]),
-                         (2, sums_a.at[pl.ds(0, GY - 1)]), (3, sums_b.at[pl.ds(0, GX - 1)])):
-        pltpu.make_async_copy(buffer, buffer, send_sem.at[slot]).wait()
+    for copy in copies:
+        copy.wait()
 
 
 def shards(theta, phi, dphi):
     vmem = pl.BlockSpec(memory_space=pltpu.VMEM)
-    cube = pltpu.VMEM((Q, N, N), F32)
+    free = pl.BlockSpec(memory_space=pl.ANY)
     halves_cube = pltpu.VMEM((Q, 2, HALF, N), F32)
     rows = pltpu.VMEM((N * ROWS, N), F32)
-    u, stress, energy = pl.pallas_call(
+    bases, pick = (jnp.asarray(c) for c in constants())
+    received, total = pl.pallas_call(
         kernel,
         out_shape=(
-            jax.ShapeDtypeStruct((Q, 8, 16, N), F32),
-            jax.ShapeDtypeStruct((3, 3), F32),
-            jax.ShapeDtypeStruct((1, 1), F32),
+            jax.ShapeDtypeStruct((N * ROWS, N), F32),
+            jax.ShapeDtypeStruct((8, N), F32),
         ),
-        in_specs=[pl.BlockSpec(memory_space=pl.ANY)] * 5,
-        out_specs=(vmem,) * 3,
+        in_specs=[free] * 5,
+        out_specs=(vmem,) * 2,
         scratch_shapes=[
             pltpu.VMEM((Q, 8, 16, N), F32),
             pltpu.VMEM((Q * Q, TABLE), F32),
             pltpu.VMEM((Q * Q, TABLE), F32),
             pltpu.VMEM((5, 2, N, N), BF16),
-            pltpu.VMEM((2, PAIRS, Q * Q), BF16),
-            rows, rows, rows, rows, cube, halves_cube, halves_cube, halves_cube,
+            pltpu.VMEM((SLOPES, Q * Q), BF16),
+            rows, rows, rows, pltpu.VMEM((Q, N, N), F32), halves_cube, halves_cube, halves_cube,
             pltpu.VMEM((Q, 2, 32, N), F32),
-            pltpu.VMEM((PAIRS * KROWS, N), F32),
-            pltpu.VMEM((4 * PAIRS, TABLE), BF16),
+            pltpu.VMEM((GROUPS * PAIRS * 8, N), F32),
+            pltpu.VMEM((4 * PAIRS + 16, TABLE), BF16),
             pltpu.VMEM((GY, 8, N), F32),
             pltpu.VMEM((GX, 8, N), F32),
             pltpu.VMEM((8, N), F32),
@@ -443,10 +529,30 @@
             pltpu.SemaphoreType.DMA((2,)),
             pltpu.SemaphoreType.DMA((2,)),
             pltpu.SemaphoreType.DMA((5,)),
+            pltpu.SemaphoreType.DMA((2, 2, GROUPS)),
         ],
         compiler_params=pltpu.CompilerParams(
             collective_id=0, has_side_effects=True, vmem_limit_bytes=56 << 20),
-    )(theta, phi.T, dphi.T, *(jnp.asarray(c) for c in constants()))
+    )(theta, phi.T, dphi.T, bases, pick)
+    u, stress, energy = pl.pallas_call(
+        finish,
+        out_shape=(
+            jax.ShapeDtypeStruct((Q, 8, 16, N), F32),
+            jax.ShapeDtypeStruct((3, 3), F32),
+            jax.ShapeDtypeStruct((1, 1), F32),
+        ),
+        in_specs=[free] * 3,
+        out_specs=(free, vmem, vmem),
+        scratch_shapes=[
+            rows,
+            pltpu.VMEM((8, N), F32),
+            pltpu.VMEM((2, N, N), BF16),
+            pltpu.VMEM((8, Q, 16, N), F32),
+            pltpu.SemaphoreType.DMA((3,)),
+            pltpu.SemaphoreType.DMA((8,)),
+        ],
+        compiler_params=pltpu.CompilerParams(vmem_limit_bytes=56 << 20),
+    )(received, total, bases)
     return u, stress, energy.reshape(())
 
 

time: 51.1 us -> 45.4 us (0.89)
  local copies, waits for them, and re-layouts: 2.55 us -> 0 us
  between operations: 2.35 us -> 0.64 us
  Pallas kernels: 46 us -> 44.6 us
    unnamed x4 -> x0, local copies, waits for them, and re-layouts: 2.55 us -> none
    pallas_call x1 -> x2, Pallas kernels: 46 us -> 44.6 us  [the longest x1 41.7 us: shards(): pl.pallas_call(kernel, out_shape=(jax.ShapeDtypeStruct((N * ROWS, N), F32...]
where the time goes in v2:
time: 45.4 us; the launch traced here: 45.2 us
  Pallas kernels  44.6 us (98%)
  between operations  0.64 us (1%)
    pallas_call x1, Pallas kernels, shards(): pl.pallas_call(kernel, out_shape=(jax.ShapeDtypeStruct((N * ROWS, N), F32...  41.7 us
    pallas_call x1, Pallas kernels, shards(): pl.pallas_call(finish, out_shape=(jax.ShapeDtypeStruct((Q, 8, 16, N), F32...  2.92 us

profile of v2, /device:TPU:1, one launch (start us, length us, event | category | flops | bytes accessed | tf_op | source)
XLA Modules:
  0.0 45.2 jit_solution(18313059278087983563)
XLA Ops:
  0.6 41.7 %shard_map.76 = (f32[1280,128]{1,0:T(8,128)}, f32[8,128]{1,0:T(8,128)}) custom-call(f32[10,8,16,128]{3,2,1,0:T(8,128)} %theta_in.1, f32[100,1024]{1,0:T(8,128)} %bitcast.3, f32[100,1024]{1,0:T(8,128)} %bitcast.4, bf16[5,2,128,128]{3,2,1,0:T(8,128)(2,1)} %constant.4.clone.bases_in, bf16[56,100]{1,0:T(8,128)(2,1)} %constant.5.clone.pick_in), custom_call_target="tpu_custom_call" | custom-call | tf_op jit(solution)/shard_map/pallas_call | solution.py:505
  42.3 2.9 %shard_map.77 = (f32[10,8,16,128]{3,2,1,0:T(8,128)}, f32[3,3]{1,0:T(4,128)}, f32[1,1]{1,0:T(1,128)}) custom-call(f32[1280,128]{1,0:T(8,128)} %get-tuple-element.8.received, f32[8,128]{1,0:T(8,128)} %get-tuple-element.9.total_in, bf16[5,2,128,128]{3,2,1,0:T(8,128)(2,1)} %constant.4.clone.bases_in), custom_call_target="tpu_custom_call" | custom-call | tf_op jit(solution)/shard_map/pallas_call | solution.py:537

commit v3 on v2

--- a/solution.py
+++ b/solution.py
@@ -18,7 +18,7 @@
 Q = 10
 GX = 16
 REGROUP = 128
-FIRST, SECOND = 64, 96
+FIRST, SECOND = 64, 112
 GY = 8
 ROWS = 10
 VALUES = 104
@@ -509,7 +509,7 @@
             jax.ShapeDtypeStruct((8, N), F32),
         ),
         in_specs=[free] * 5,
-        out_specs=(vmem,) * 2,
+        out_specs=(free, vmem),
         scratch_shapes=[
             pltpu.VMEM((Q, 8, 16, N), F32),
             pltpu.VMEM((Q * Q, TABLE), F32),

time: 45.4 us -> 44.5 us (0.980)
  Pallas kernels: 44.6 us -> 43.7 us
    pallas_call x1, Pallas kernels: 41.7 us -> 40.8 us  [shards(): pl.pallas_call(kernel, out_shape=(jax.ShapeDtypeStruct((N * ROWS, N), F32...]
where the time goes in v3:
time: 44.5 us; the launch traced here: 44.3 us
  Pallas kernels  43.7 us (98%)
  between operations  0.64 us (1%)
    pallas_call x1, Pallas kernels, shards(): pl.pallas_call(kernel, out_shape=(jax.ShapeDtypeStruct((N * ROWS, N), F32...  40.8 us
    pallas_call x1, Pallas kernels, shards(): pl.pallas_call(finish, out_shape=(jax.ShapeDtypeStruct((Q, 8, 16, N), F32...  2.92 us

profile of v3, /device:TPU:1, one launch (start us, length us, event | category | flops | bytes accessed | tf_op | source)
XLA Modules:
  0.0 44.3 jit_solution(1302493209669685168)
XLA Ops:
  0.6 40.8 %shard_map.76 = (f32[1280,128]{1,0:T(8,128)}, f32[8,128]{1,0:T(8,128)}) custom-call(f32[10,8,16,128]{3,2,1,0:T(8,128)} %theta_in.1, f32[100,1024]{1,0:T(8,128)} %bitcast.3, f32[100,1024]{1,0:T(8,128)} %bitcast.4, bf16[5,2,128,128]{3,2,1,0:T(8,128)(2,1)} %constant.4.clone.bases_in, bf16[56,100]{1,0:T(8,128)(2,1)} %constant.5.clone.pick_in), custom_call_target="tpu_custom_call" | custom-call | tf_op jit(solution)/shard_map/pallas_call | solution.py:505
  41.4 2.9 %shard_map.77 = (f32[10,8,16,128]{3,2,1,0:T(8,128)}, f32[3,3]{1,0:T(4,128)}, f32[1,1]{1,0:T(1,128)}) custom-call(f32[1280,128]{1,0:T(8,128)} %get-tuple-element.8.received, f32[8,128]{1,0:T(8,128)} %get-tuple-element.9.total_in, bf16[5,2,128,128]{3,2,1,0:T(8,128)(2,1)} %constant.4.clone.bases_in), custom_call_target="tpu_custom_call" | custom-call | tf_op jit(solution)/shard_map/pallas_call | solution.py:537

commit v4 on v3

--- a/solution.py
+++ b/solution.py
@@ -455,27 +455,13 @@
         pltpu.make_async_copy(buffer, buffer, send_sem.at[slot]).wait()
 
 
-def finish(received, total_in, bases_in, u_out, stress_out, energy_out, rows_in, total, bases, u, in_sem, out_sem):
+def finish(received, total_in, bases_in, u_out, stress_hbm, energy_hbm,
+           rows_in, total, bases, u, stress_out, energy_out, in_sem, out_sem):
     inputs = [pltpu.make_async_copy(source, target, in_sem.at[i]) for i, (source, target) in enumerate(
         ((received, rows_in), (bases_in.at[0], bases), (total_in, total)))]
     for copy in inputs:
         copy.start()
-    for copy in inputs:
-        copy.wait()
-    zbh, zbl = bases[0], bases[1]
-    for r in range(2):
-        block = rows_in[pl.ds(8 + r, N, stride=ROWS), :].T
-        out = mm3(split(block), (zbh, zbl)).reshape(4, 2, 16, N)
-        for b in range(4):
-            for q in range(2):
-                u[2 * b + r, 8 + q] = out[b, q]
-    copies = []
-    for x in range(8):
-        block = rows_in[pl.ds(x, N, stride=ROWS), :].T
-        u[x, 0:8] = mm3(split(block), (zbh, zbl)).reshape(8, 16, N)
-        copies.append(pltpu.make_async_copy(u.at[x], u_out.at[:, x], out_sem.at[x]))
-        copies[-1].start()
-
+    inputs[2].wait()
     cells = float(N) ** 3
     wave = (2.0 * math.pi / N) ** 2
     sums = jnp.sum(total[...], axis=1, keepdims=True)
@@ -492,6 +478,26 @@
         here = ((r3 == a) & (c3 == b)) | ((r3 == b) & (c3 == a))
         stress = jnp.where(here, pick_sum(r + 1) * (-0.5 * wave / cells), stress)
     stress_out[...] = stress
+    copies = [pltpu.make_async_copy(stress_out, stress_hbm, out_sem.at[8]),
+              pltpu.make_async_copy(energy_out, energy_hbm, out_sem.at[9])]
+    for copy in copies:
+        copy.start()
+
+    inputs[0].wait()
+    inputs[1].wait()
+    zbh, zbl = bases[0], bases[1]
+    for r in range(2):
+        block = rows_in[pl.ds(8 + r, N, stride=ROWS), :].T
+        out = mm3(split(block), (zbh, zbl)).reshape(4, 2, 16, N)
+        for b in range(4):
+            for q in range(2):
+                u[2 * b + r, 8 + q] = out[b, q]
+    for x in range(8):
+        block = rows_in[pl.ds(x, N, stride=ROWS), :].T
+        u[x, 0:8] = mm3(split(block), (zbh, zbl)).reshape(8, 16, N)
+        copies.append(pltpu.make_async_copy(u.at[x], u_out.at[:, x], out_sem.at[x]))
+        copies[-1].start()
+
     for copy in copies:
         copy.wait()
 
@@ -542,14 +548,16 @@
             jax.ShapeDtypeStruct((1, 1), F32),
         ),
         in_specs=[free] * 3,
-        out_specs=(free, vmem, vmem),
+        out_specs=(free,) * 3,
         scratch_shapes=[
             rows,
             pltpu.VMEM((8, N), F32),
             pltpu.VMEM((2, N, N), BF16),
             pltpu.VMEM((8, Q, 16, N), F32),
+            pltpu.VMEM((3, 3), F32),
+            pltpu.VMEM((1, 1), F32),
             pltpu.SemaphoreType.DMA((3,)),
-            pltpu.SemaphoreType.DMA((8,)),
+            pltpu.SemaphoreType.DMA((10,)),
         ],
         compiler_params=pltpu.CompilerParams(vmem_limit_bytes=56 << 20),
     )(received, total, bases)

time: 44.5 us -> 43.9 us (0.987)
  Pallas kernels: 43.7 us -> 43.1 us
    pallas_call x1, Pallas kernels: 2.92 us -> 2.36 us  [shards(): pl.pallas_call(finish, out_shape=(jax.ShapeDtypeStruct((Q, 8, 16, N), F32...]
where the time goes in v4:
time: 43.9 us; the launch traced here: 43.8 us
  Pallas kernels  43.1 us (98%)
  between operations  0.64 us (1%)
    pallas_call x1, Pallas kernels, shards(): pl.pallas_call(kernel, out_shape=(jax.ShapeDtypeStruct((N * ROWS, N), F32...  40.8 us
    pallas_call x1, Pallas kernels, shards(): pl.pallas_call(finish, out_shape=(jax.ShapeDtypeStruct((Q, 8, 16, N), F32...  2.36 us

profile of v4, /device:TPU:1, one launch (start us, length us, event | category | flops | bytes accessed | tf_op | source)
XLA Modules:
  0.0 43.8 jit_solution(11906466454648911232)
XLA Ops:
  0.6 40.8 %shard_map.76 = (f32[1280,128]{1,0:T(8,128)}, f32[8,128]{1,0:T(8,128)}) custom-call(f32[10,8,16,128]{3,2,1,0:T(8,128)} %theta_in.1, f32[100,1024]{1,0:T(8,128)} %bitcast.3, f32[100,1024]{1,0:T(8,128)} %bitcast.4, bf16[5,2,128,128]{3,2,1,0:T(8,128)(2,1)} %constant.4.clone.bases_in, bf16[56,100]{1,0:T(8,128)(2,1)} %constant.5.clone.pick_in), custom_call_target="tpu_custom_call" | custom-call | tf_op jit(solution)/shard_map/pallas_call | solution.py:511
  41.4 2.4 %shard_map.77 = (f32[10,8,16,128]{3,2,1,0:T(8,128)}, f32[3,3]{1,0:T(4,128)}, f32[1,1]{1,0:T(1,128)}) custom-call(f32[1280,128]{1,0:T(8,128)} %get-tuple-element.8.received, f32[8,128]{1,0:T(8,128)} %get-tuple-element.9.total_in, bf16[5,2,128,128]{3,2,1,0:T(8,128)(2,1)} %constant.4.clone.bases_in), custom_call_target="tpu_custom_call" | custom-call | tf_op jit(solution)/shard_map/pallas_call | solution.py:543

commit v5 on v4

--- a/solution.py
+++ b/solution.py
@@ -98,6 +98,20 @@
             values[i | bit] = jnp.where(low, pltpu.roll(first, N - step, axis), second)
         bit *= 2
     return values
+
+
+def exchange_all(values, lane_step):
+    count = len(values)
+    axis = values[0].ndim - 1
+    lane = lax.broadcasted_iota(jnp.int32, values[0].shape, axis)
+    turned = [pltpu.roll(value, i * lane_step, axis) if i else value for i, value in enumerate(values)]
+    turned = [turned[-i % count] for i in range(count)]
+    bit = 1
+    while bit < count:
+        here = (lane & (bit * lane_step)) != 0
+        turned = [jnp.where(here, turned[(i - bit) % count], turned[i]) for i in range(count)]
+        bit *= 2
+    return [pltpu.roll(value, N - i * lane_step, axis) if i else value for i, value in enumerate(turned)]
 
 
 def kernel(theta_in, phi_in, dphi_in, bases_in, pick_in, r2, total_out,
@@ -225,7 +239,7 @@
     pl.semaphore_wait(barrier, N - 1)
 
     def send1(i, c):
-        to = lax.rem(plane + i, N)
+        to = lax.rem(plane + i * 3, N)
         pltpu.make_async_remote_copy(
             s1.at[pl.ds(to * ROWS, ROWS)], r1.at[pl.ds(place_in_order * ROWS, ROWS)], send_sem.at[0], recv_sem.at[0],
             device_id=(to // GY, lax.rem(to, GY)), device_id_type=MESH).start()
@@ -272,7 +286,7 @@
 
     def regroup(tile, c):
         place = pl.ds(pl.multiple_of(tile * REGROUP, REGROUP), REGROUP)
-        main = exchange([mid[i, place] for i in range(8)], 16)
+        main = exchange_all([mid[i, place] for i in range(8)], 16)
         ends = exchange([mid[i, place] for i in (8, 9)], 16)
         for i, value in enumerate(main + ends):
             mid[i, place] = value
@@ -324,7 +338,7 @@
                 s2[pl.ds((2 * a + h) * GX * ROWS + 8 + r, GX, stride=ROWS), :] = ends[a][r * GX:(r + 1) * GX]
 
     def send2(i, c):
-        to = lax.rem(plane + i, N)
+        to = lax.rem(plane + i * 3, N)
         to_x, to_y = to // GY, lax.rem(to, GY)
         pltpu.make_async_remote_copy(
             s2.at[pl.ds((to_y * GX + to_x) * ROWS, ROWS)], r2.at[pl.ds(plane * ROWS, ROWS)], send_sem.at[1], recv_sem.at[1],

time: 43.9 us -> 43.7 us (level)
  no operation moved by 1% of the time
where the time goes in v5:
time: 43.7 us; the launch traced here: 43.5 us
  Pallas kernels  42.9 us (98%)
  between operations  0.64 us (1%)
    pallas_call x1, Pallas kernels, shards(): pl.pallas_call(kernel, out_shape=(jax.ShapeDtypeStruct((N * ROWS, N), F32...  40.5 us
    pallas_call x1, Pallas kernels, shards(): pl.pallas_call(finish, out_shape=(jax.ShapeDtypeStruct((Q, 8, 16, N), F32...  2.36 us

profile of v5, /device:TPU:1, one launch (start us, length us, event | category | flops | bytes accessed | tf_op | source)
XLA Modules:
  0.0 43.5 jit_solution(937816683190887232)
XLA Ops:
  0.6 40.5 %shard_map.76 = (f32[1280,128]{1,0:T(8,128)}, f32[8,128]{1,0:T(8,128)}) custom-call(f32[10,8,16,128]{3,2,1,0:T(8,128)} %theta_in.1, f32[100,1024]{1,0:T(8,128)} %bitcast.3, f32[100,1024]{1,0:T(8,128)} %bitcast.4, bf16[5,2,128,128]{3,2,1,0:T(8,128)(2,1)} %constant.4.clone.bases_in, bf16[56,100]{1,0:T(8,128)(2,1)} %constant.5.clone.pick_in), custom_call_target="tpu_custom_call" | custom-call | tf_op jit(solution)/shard_map/pallas_call | solution.py:525
  41.2 2.4 %shard_map.77 = (f32[10,8,16,128]{3,2,1,0:T(8,128)}, f32[3,3]{1,0:T(4,128)}, f32[1,1]{1,0:T(1,128)}) custom-call(f32[1280,128]{1,0:T(8,128)} %get-tuple-element.8.received, f32[8,128]{1,0:T(8,128)} %get-tuple-element.9.total_in, bf16[5,2,128,128]{3,2,1,0:T(8,128)(2,1)} %constant.4.clone.bases_in), custom_call_target="tpu_custom_call" | custom-call | tf_op jit(solution)/shard_map/pallas_call | solution.py:557

commit v6 on v5

--- a/solution.py
+++ b/solution.py
@@ -116,7 +116,7 @@
 
 def kernel(theta_in, phi_in, dphi_in, bases_in, pick_in, r2, total_out,
            theta, phi, dphi, bases, pick, s1, r1, s2, mid, spec, uspec, grad, partner, ktab, tabs, sums_a, sums_b, part,
-           send_sem, recv_sem, own_sem, sib_sem, sum_sem, in_sem, tab_sem):
+           send_sem, recv_sem, own_sem, sib_sem, sum_sem, in_sem, tab_sem, total_here):
     inputs = [pltpu.make_async_copy(source, target, in_sem.at[i]) for i, (source, target) in enumerate(
         ((theta_in, theta), (bases_in, bases), (phi_in, phi), (dphi_in, dphi), (pick_in, pick)))]
     for copy in inputs:
@@ -458,11 +458,14 @@
     total = sums_b[0]
     for i in range(1, GX):
         total = total + sums_b[i]
-    total_out[...] = total
+    total_here[...] = total
+    total_copy = pltpu.make_async_copy(total_here, total_out, in_sem.at[4])
+    total_copy.start()
 
     got = r2.at[all_but_one]
     pltpu.make_async_copy(got, got, recv_sem.at[1]).wait()
     own2.wait()
+    total_copy.wait()
 
     for slot, buffer in ((0, s1.at[all_but_one]), (1, s2.at[all_but_one]),
                          (2, sums_a.at[pl.ds(0, GY - 1)]), (3, sums_b.at[pl.ds(0, GX - 1)])):
@@ -529,7 +532,7 @@
             jax.ShapeDtypeStruct((8, N), F32),
         ),
         in_specs=[free] * 5,
-        out_specs=(free, vmem),
+        out_specs=(free, free),
         scratch_shapes=[
             pltpu.VMEM((Q, 8, 16, N), F32),
             pltpu.VMEM((Q * Q, TABLE), F32),
@@ -550,6 +553,7 @@
             pltpu.SemaphoreType.DMA((2,)),
             pltpu.SemaphoreType.DMA((5,)),
             pltpu.SemaphoreType.DMA((2, 2, GROUPS)),
+            pltpu.VMEM((8, N), F32),
         ],
         compiler_params=pltpu.CompilerParams(
             collective_id=0, has_side_effects=True, vmem_limit_bytes=56 << 20),

time: 43.7 us -> 43.3 us (level)
  no operation moved by 1% of the time
where the time goes in v6:
time: 43.3 us; the launch traced here: 43.2 us
  Pallas kernels  42.6 us (98%)
  between operations  0.64 us (1%)
    pallas_call x1, Pallas kernels, shards(): pl.pallas_call(kernel, out_shape=(jax.ShapeDtypeStruct((N * ROWS, N), F32...  40.2 us
    pallas_call x1, Pallas kernels, shards(): pl.pallas_call(finish, out_shape=(jax.ShapeDtypeStruct((Q, 8, 16, N), F32...  2.36 us

profile of v6, /device:TPU:1, one launch (start us, length us, event | category | flops | bytes accessed | tf_op | source)
XLA Modules:
  0.0 43.2 jit_solution(13870805284280943286)
XLA Ops:
  0.6 40.2 %shard_map.76 = (f32[1280,128]{1,0:T(8,128)}, f32[8,128]{1,0:T(8,128)}) custom-call(f32[10,8,16,128]{3,2,1,0:T(8,128)} %theta_in.1, f32[100,1024]{1,0:T(8,128)} %bitcast.3, f32[100,1024]{1,0:T(8,128)} %bitcast.4, bf16[5,2,128,128]{3,2,1,0:T(8,128)(2,1)} %constant.4.clone.bases_in, bf16[56,100]{1,0:T(8,128)(2,1)} %constant.5.clone.pick_in), custom_call_target="tpu_custom_call" | custom-call | tf_op jit(solution)/shard_map/pallas_call | solution.py:528
  40.8 2.4 %shard_map.77 = (f32[10,8,16,128]{3,2,1,0:T(8,128)}, f32[3,3]{1,0:T(4,128)}, f32[1,1]{1,0:T(1,128)}) custom-call(f32[1280,128]{1,0:T(8,128)} %get-tuple-element.8.received, f32[8,128]{1,0:T(8,128)} %get-tuple-element.9.total_in, bf16[5,2,128,128]{3,2,1,0:T(8,128)(2,1)} %constant.4.clone.bases_in), custom_call_target="tpu_custom_call" | custom-call | tf_op jit(solution)/shard_map/pallas_call | solution.py:561
